TPU v7x, 1024 devices: a whole 8x8x8 slice. The times are simulated.
1024 devices in a mesh: row: 8 (over y), col: 128 (over z, x, core).
Axes of the slice: x: 8, y: 8, z: 8, core: 2. Of those that a mesh axis runs over, the one named last changes fastest.
Arguments:
- pivot: float32 [1024, 1024], replicated, may hold values from -1 to 2
- col_panel: float32 [4096, 1024], P('row', 'col'), may hold values from -0.25 to 0.25
- row_panel: float32 [1024, 32768], P('row', 'col'), may hold values from -6 to 6
- trailing: float32 [4096, 32768], P('row', 'col'), may hold values from -6 to 6
Outputs:
- updated: float32 [4096, 32768], P('row', 'col')
All inputs are finite; a program needn't handle non-finite values.
Results may differ from a plain program's by a relative error of at most 0.000061.
Values sent between devices are 32-bit elements; how exact they have to be, the bound alone decides.
A program may use at most 64 MiB of HBM per device.

v0:
```python
import jax
import jax.numpy as jnp
from jax import lax
from jax.sharding import PartitionSpec as P

B = 512


def sent_to_all(value, axis):
    copies = jnp.broadcast_to(value, (lax.axis_size(axis), *value.shape))
    return lax.all_to_all(copies, axis, split_axis=0, concat_axis=0, tiled=True)


def joined_along(pieces, dim):
    lengths = list(pieces.shape[1:])
    lengths[dim] *= pieces.shape[0]
    return jnp.moveaxis(pieces, 0, dim).reshape(lengths)


def collect(value, axis, dim):
    pieces = sent_to_all(value, axis)
    return joined_along(pieces, dim)


def product(left, right):
    return jnp.dot(left, right, precision=lax.Precision.HIGHEST, preferred_element_type=jnp.float32)


def newton_inverse(matrix):
    identity = jnp.eye(matrix.shape[0], dtype=jnp.float32)
    initial = 2.0 * identity - matrix
    return product(initial, 2.0 * identity - product(matrix, initial))


def local(pivot, col_panel, row_panel, trailing):
    gathered_cols = lax.all_gather(col_panel, "col", axis=1, tiled=True)
    gathered_rows = collect(row_panel, "row", 0)
    top_left = pivot[:B, :B]
    top_right = pivot[:B, B:]
    low_left = pivot[B:, :B]
    low_right = pivot[B:, B:]
    inverse_one = newton_inverse(top_left)
    multiplier = product(low_left, inverse_one)
    schur = low_right - product(multiplier, top_right)
    inverse_two = newton_inverse(schur)
    factor_one = product(gathered_cols[:, :B], inverse_one)
    factor_two = product(gathered_cols[:, B:] - product(factor_one, top_right), inverse_two)
    first_rows = gathered_rows[:B]
    rows_two = gathered_rows[B:] - product(multiplier, first_rows)
    return trailing - product(factor_one, first_rows) - product(factor_two, rows_two)


def solution(mesh):
    return jax.shard_map(
        local,
        mesh=mesh,
        in_specs=(P(), P("row", "col"), P("row", "col"), P("row", "col")),
        out_specs=P("row", "col"),
        check_vma=False,
    )
```

profile of v0, /device:TPU:1, one launch (start us, length us, event | category | flops | bytes accessed | tf_op | source)
XLA Modules:
  0.0 134.1 jit_solution(1211038839914729375)
XLA Ops:
  6.5 0.0 all-gather.2.cloned.1.call-start
  6.5 0.7 all-gather.2.cloned.1.call-update
  7.3 2.0 %broadcast_in_dim.3 = f32[8,128,256]{2,1,0:T(8,128)} broadcast(f32[128,256]{1,0:T(8,128)} %param.6), dimensions={1,2} | broadcast | bytes 1179648 | tf_op jit(solution)/shard_map/broadcast_in_dim | solution.py:10
  9.2 8.1 %all-to-all-start = ((f32[8,128,256]{2,1,0:T(8,128)}), f32[8,128,256]{2,1,0:T(8,128)}, u32[]{:S(2)}, u32[]{:S(2)}) async-start(f32[8,128,256]{2,1,0:T(8,128)} %broadcast_in_dim.3), calls=%async_computation | async-start | bytes 2097152 | tf_op jit(solution)/shard_map/all_to_all | solution.py:11
  17.3 0.0 copy-start.1
  17.3 3.6 %select_subtract_fusion.2 = f32[512,512]{1,0:T(8,128)S(1)} fusion(f32[1024,1024]{1,0:T(8,128)} %param.4), kind=kOutput, calls=%fused_computation.2 | convolution fusion | flops 1612185600 | bytes 3145728 | tf_op jit(solution)/shard_map/dot_general | solution.py:26
  21.0 3.1 %fusion = f32[512,512]{1,0:T(8,128)S(1)} fusion(f32[512,512]{1,0:T(8,128)S(1)} %select_subtract_fusion.2, f32[1024,1024]{1,0:T(8,128)} %param.4), kind=kOutput, calls=%fused_computation.7 | convolution fusion | flops 1611399168 | bytes 3145728 | tf_op jit(solution)/shard_map/dot_general | solution.py:26
  24.1 0.0 copy-done.1
  24.1 3.5 %fusion.4 = f32[512,512]{1,0:T(8,128)S(1)} fusion(f32[512,512]{1,0:T(8,128)S(1)} %fusion, f32[1024,1024]{1,0:T(8,128)S(1)} %copy-done.1), kind=kOutput, calls=%fused_computation.14 | convolution fusion | flops 1610612736 | bytes 3145728 | tf_op jit(solution)/shard_map/dot_general | solution.py:26
  27.6 1.8 %convolution_subtract_fusion = f32[512,512]{1,0:T(8,128)S(1)} fusion(f32[512,512]{1,0:T(8,128)S(1)} %fusion.4, f32[1024,1024]{1,0:T(8,128)S(1)} %copy-done.1), kind=kOutput, calls=%fused_computation.4 | convolution fusion | flops 1610874880 | bytes 4194304 | tf_op jit(solution)/shard_map/dot_general | solution.py:26
  29.4 1.9 %select_subtract_fusion = f32[512,512]{1,0:T(8,128)S(1)} fusion(f32[512,512]{1,0:T(8,128)S(1)} %convolution_subtract_fusion), kind=kOutput, calls=%fused_computation | convolution fusion | flops 1612185600 | bytes 2097152 | tf_op jit(solution)/shard_map/dot_general | solution.py:26
  31.3 3.1 %fusion.1 = f32[512,512]{1,0:T(8,128)} fusion(f32[512,512]{1,0:T(8,128)S(1)} %select_subtract_fusion, f32[512,512]{1,0:T(8,128)S(1)} %convolution_subtract_fusion), kind=kOutput, calls=%fused_computation.8 | convolution fusion | flops 1611399168 | bytes 3145728 | tf_op jit(solution)/shard_map/dot_general | solution.py:26
  34.4 0.0 all-to-all-done
  34.4 1.3 fusion.26
  35.7 1.8 %convolution_subtract_fusion.3 = f32[512,256]{1,0:T(8,128)S(1)} fusion(f32[512,256]{1,0:T(8,128)S(1)} %bitcast.23, f32[512,512]{1,0:T(8,128)S(1)} %fusion.4, f32[512,256]{1,0:T(8,128)S(1)} %bitcast.21), kind=kOutput, calls=%fused_computation.10 | convolution fusion | flops 805437440 | bytes 2621440 | tf_op jit(solution)/shard_map/dot_general | solution.py:26
  37.5 76.8 %all-gather.2.cloned.1.call-done = f32[512,1024]{0,1:T(8,128)} async-done(((f32[512,8]{0,1:T(8,128)}), f32[512,1024]{0,1:T(8,128)}) %all-gather.2.cloned.1.call-update) | async-done | bytes 2097168 | tf_op jit(solution)/shard_map/all_gather | solution.py:36
  114.3 0.0 copy-start.2
  114.3 3.2 %fusion.2 = f32[512,512]{1,0:T(8,128)S(1)} fusion(f32[512,512]{1,0:T(8,128)S(1)} %fusion, f32[512,1024]{0,1:T(8,128)} %all-gather.2.cloned.1.call-done), kind=kOutput, calls=%fused_computation.12 | convolution fusion | flops 1610612736 | bytes 3145728 | tf_op jit(solution)/shard_map/dot_general | solution.py:26
  117.6 0.0 copy-start
  117.6 2.9 %convolution_subtract_fusion.4 = f32[512,256]{1,0:T(8,128)S(1)} fusion(f32[512,256]{1,0:T(8,128)} %param.7, f32[512,512]{1,0:T(8,128)S(1)} %fusion.2, f32[512,256]{1,0:T(8,128)S(1)} %bitcast.22), kind=kOutput, calls=%fused_computation.11 | convolution fusion | flops 805437440 | bytes 2621440 | tf_op jit(solution)/shard_map/dot_general | solution.py:26
  120.5 0.0 copy-done.2
  120.5 3.1 %convolution_subtract_fusion.1 = f32[512,512]{0,1:T(8,128)S(1)} fusion(f32[512,512]{1,0:T(8,128)S(1)} %fusion.2, f32[512,1024]{0,1:T(8,128)S(1)} %copy-done.2, f32[1024,1024]{1,0:T(8,128)} %param.4), kind=kOutput, calls=%fused_computation.5 | convolution fusion | flops 1610874880 | bytes 4194304 | tf_op jit(solution)/shard_map/dot_general | solution.py:26
  123.6 0.0 copy-done
  123.6 1.8 %fusion.27 = f32[512,512]{1,0:T(8,128)S(1)} fusion(f32[512,512]{0,1:T(8,128)S(1)} %convolution_subtract_fusion.1, f32[512,512]{1,0:T(8,128)S(1)} %copy-done), kind=kOutput, calls=%fused_computation.38 | convolution fusion | flops 1610612736 | bytes 3145728 | tf_op jit(solution)/shard_map/dot_general | solution.py:26
  125.5 1.8 %convolution_subtract_fusion.2 = f32[512,256]{1,0:T(8,128)} fusion(f32[512,256]{1,0:T(8,128)S(1)} %convolution_subtract_fusion.4, f32[512,512]{1,0:T(8,128)S(1)} %fusion.27, f32[512,256]{1,0:T(8,128)S(1)} %convolution_subtract_fusion.3), kind=kOutput, calls=%fused_computation.9 | convolution fusion | flops 805437440 | bytes 2621440 | tf_op jit(solution)/shard_map/dot_general | solution.py:26
Async XLA Ops:
  6.5 107.8 %all-gather.2.cloned.1.call-start = ((), (), s32[]{:S(2)}) async-start(), calls=%async_computation.1 | async-start | bytes 2113536 | tf_op jit(solution)/shard_map/all_gather | solution.py:36
  9.2 25.2 %all-to-all-start = ((f32[8,128,256]{2,1,0:T(8,128)}), f32[8,128,256]{2,1,0:T(8,128)}, u32[]{:S(2)}, u32[]{:S(2)}) async-start(f32[8,128,256]{2,1,0:T(8,128)} %broadcast_in_dim.3), calls=%async_computation | async-start | bytes 2097152 | tf_op jit(solution)/shard_map/all_to_all | solution.py:11
  17.3 6.8 %copy-start.1 = (f32[1024,1024]{1,0:T(8,128)S(1)}, f32[1024,1024]{1,0:T(8,128)}, u32[]{:S(2)}) copy-start(f32[1024,1024]{1,0:T(8,128)} %param.4) | copy-start | bytes 12582916
  114.3 6.2 %copy-start.2 = (f32[512,1024]{0,1:T(8,128)S(1)}, f32[512,1024]{0,1:T(8,128)}, u32[]{:S(2)}) copy-start(f32[512,1024]{0,1:T(8,128)} %all-gather.2.cloned.1.call-done) | copy-start | bytes 6291460
  117.6 6.1 %copy-start = (f32[512,512]{1,0:T(8,128)S(1)}, f32[512,512]{1,0:T(8,128)}, u32[]{:S(2)}) copy-start(f32[512,512]{1,0:T(8,128)} %fusion.1) | copy-start | bytes 3145732
Sparse Core Ops, SparseCore 0:
  11.6 102.6 all-gather.1
where the time goes:
time: 134 us
  waiting for transfers between devices  77.5 us (58%)
  matrix products  31.7 us (24%)
  between operations  13.5 us (10%)
  starting transfers between devices  8.11 us (6%)
  local copies, waits for them, and re-layouts  3.26 us (2%)
    all_gather x1, waiting for transfers between devices, local(): gathered_cols = lax.all_gather(col_panel, 'col', axis=1, tiled=True)  76.8 us
    dot_general x12, matrix products, product(): jnp.dot(left, right, precision=lax.Precision.HIGHEST, preferred_element_t...  31.7 us
    all_to_all x1, starting transfers between devices, sent_to_all(): return lax.all_to_all(copies, axis, split_axis=0, concat_axis=0, tiled=True)  8.11 us
  transfers between devices with their start and end apart: 2, of which 1 were waited for; matrix products, arithmetic and copies ran while one was open for 16% of the time, Pallas kernels for 0%

commit v1 on v0

v1 whole, which is shorter than its diff:
```python
import jax
import jax.numpy as jnp
from jax import lax
from jax.experimental import pallas as pl
from jax.experimental.pallas import tpu as pltpu
from jax.sharding import PartitionSpec as P

B = 512
N = 8
MESH = pl.DeviceIdType.MESH
F32 = jnp.float32
BF16 = jnp.bfloat16
GROUPS = ((0, 4), (4, 2), (6, 1), (7, 1))


def split(value):
    high = value.astype(BF16)
    return high, (value - high.astype(F32)).astype(BF16)


def dot(left, right):
    return jnp.dot(left, right, preferred_element_type=F32)


def product(left, right):
    return dot(left[0], right[0]) + (dot(left[0], right[1]) + dot(left[1], right[0]))


def kernel(pivot_ref, col_ref, row_ref, trail_ref, out_ref, piv, rb, cb, trail, f_a, f_b, h_a, h_b, h_inv1, h_n, h_ll, h_inv2, h_y,
           loc, zs, zr, xs, xr, bs, br, rs, rr, inz, inx, iny, ins):
    y = lax.axis_index("row")
    col = lax.axis_index("col")
    c = lax.rem(col, 2)
    x = lax.rem(col // 2, N)
    z = col // (2 * N)

    def column(z_, x_, c_):
        return (z_ * N + x_) * 2 + c_

    def first(y_, z_, x_, c_):
        return jnp.where((y_ == 0) & (z_ == 0) & (x_ == 0) & (c_ == 0), 100, 0)

    def ringed(v):
        return 2 * jnp.minimum(v, N - v) - jnp.where(v < N // 2, 1, 0)

    mine = first(y, z, x, c)
    partners = []
    zp, xp, yp = [], [], []
    for k in range(N):
        zp.append((y, column(k, x, c)))
        partners.append((zp[k], z != k, k + first(y, k, x, c) > z + mine, inz.at[z], inz.at[k]))
    for k in range(N):
        xp.append((y, column(z, k, c)))
        partners.append((xp[k], x != k, ringed(jnp.int32(k)) + first(y, z, k, c) > ringed(x) + mine, inx.at[x], inx.at[k]))
    for k, off in enumerate((1, N - 1, 2, N - 2)):
        other = lax.rem(y + off, N)
        yp.append((other, col))
        partners.append((yp[k], None, ringed(other) + first(other, z, x, c) > ringed(y) + mine, iny.at[k ^ 1], iny.at[k]))
    sib = (y, column(z, x, 1 - c))
    partners.append((sib, None, (c == 1), ins.at[0], ins.at[0]))

    def both(a, b):
        return b if a is None else a & b

    local = []
    for k, (r, q) in enumerate(((0, 0), (0, 1), (1, 0), (1, 1))):
        part = (pl.ds(r * B, B), pl.ds(q * B, B))
        local.append(pltpu.make_async_copy(pivot_ref.at[part], piv.at[part], loc.at[k]))
    own_c = pltpu.make_async_copy(col_ref, cb.at[z, x, c], loc.at[4])
    own_r = pltpu.make_async_copy(row_ref, rb.at[y], loc.at[5])
    own_t = pltpu.make_async_copy(trail_ref, trail, loc.at[6])
    own_c.start()
    local[0].start()

    barrier = pltpu.get_barrier_semaphore()
    count = jnp.int32(0)
    for dev, there, later, _, _ in partners:
        earlier = both(there, jnp.logical_not(later))
        count = count + earlier.astype(jnp.int32)

        @pl.when(both(there, later))
        def _():
            pl.semaphore_signal(barrier, inc=1, device_id=dev, device_id_type=MESH)

    @pl.when(count > 0)
    def _():
        pl.semaphore_wait(barrier, count)

    def remote(src, dst, send, recv, dev):
        return pltpu.make_async_remote_copy(src_ref=src, dst_ref=dst, send_sem=send, recv_sem=recv, device_id=dev, device_id_type=MESH)

    def z_copy(k, src_z=None):
        return remote(col_ref, cb.at[z, x, c], zs.at[k], zr.at[z], zp[k])

    def z_wait(k):
        remote(col_ref, cb.at[k, x, c], zs.at[k], zr.at[k], zp[k]).wait_recv()

    for k in range(N):
        _, there, later, _, _ = partners[k]

        @pl.when(there & jnp.logical_not(later))
        def _():
            z_copy(k).start()

    for dev, there, later, theirs, _ in partners:
        @pl.when(both(there, jnp.logical_not(later)))
        def _():
            pl.semaphore_signal(theirs, inc=1, device_id=dev, device_id_type=MESH)

    def admit(i):
        _, there, later, _, own = partners[i]

        @pl.when(both(there, later))
        def _():
            pl.semaphore_wait(own, 1)

    for k in range(1, 4):
        local[k].start()
    own_r.start()
    own_t.start()

    half = B // 8

    def r_copy(k):
        src_y = lax.rem(y + (0, 0, 0, 0, N - 2, 2, N - 2, 2)[k], N)
        dev = yp[(0, 1, 2, 3, 0, 1, 2, 3)[k]]
        if k < 4:
            src, dst = row_ref, rb.at[y]
        elif k < 6:
            src = dst = rb.at[src_y]
        else:
            src = dst = rb.at[src_y, pl.ds((k - 6) * half, half)]
        return remote(src, dst, rs.at[k], rr.at[k], dev)

    def r_wait(k):
        at = lax.rem(y + (N - 1, 1, N - 2, 2, N - 3, 3, N - 4, 4)[k], N)
        ref = rb.at[at] if k < 6 else rb.at[at, pl.ds((k - 6) * half, half)]
        remote(ref, ref, rs.at[k], rr.at[k], yp[0]).wait_recv()

    for k in (2, 3, 0, 1):
        admit(2 * N + k)
        r_copy(k).start()
    admit(2 * N + 4)

    eye = (lax.broadcasted_iota(jnp.int32, (B, B), 0) == lax.broadcasted_iota(jnp.int32, (B, B), 1)).astype(F32)

    def load(ref):
        return ref[0], ref[1]

    def store(ref, value):
        ref[0], ref[1] = split(value)

    local[0].wait()
    e = eye - piv[:B, :B]
    f_a[...] = e
    store(h_a, e)
    square = product(load(h_a), load(h_a))
    f_b[...] = square
    store(h_b, square)
    store(h_inv1, eye + f_a[...] + f_b[...] + product(load(h_a), load(h_b)))
    local[1].wait()
    store(h_n, product(load(h_inv1), split(piv[:B, B:])))
    local[2].wait()
    local[3].wait()
    store(h_ll, piv[B:, :B])
    e = eye - piv[B:, B:] + product(load(h_ll), load(h_n))
    f_a[...] = e
    store(h_a, e)
    r_wait(2)
    r_copy(4).start()
    r_copy(6).start()
    r_wait(3)
    r_copy(5).start()
    r_copy(7).start()
    square = product(load(h_a), load(h_a))
    f_b[...] = square
    store(h_b, square)
    store(h_inv2, eye + f_a[...] + f_b[...] + product(load(h_a), load(h_b)))

    own_c.wait()
    for k in range(N):
        admit(N + k)

    def x_copy(g, k):
        z0, n = GROUPS[g]
        ref = cb.at[pl.ds(z0, n), x, c]
        return remote(ref, ref, xs.at[g, k], xr.at[g, x], xp[k])

    def x_wait(g, k):
        z0, n = GROUPS[g]
        ref = cb.at[pl.ds(z0, n), k, c]
        remote(ref, ref, xs.at[g, k], xr.at[g, k], xp[k]).wait_recv()

    for g, (z0, n) in enumerate(GROUPS):
        for k in range(z0, z0 + n):
            _, there, later, _, own = partners[k]

            @pl.when(there & later)
            def _():
                pl.semaphore_wait(own, 1)
                z_copy(k).start()

            @pl.when(there)
            def _():
                z_wait(k)

        for k in range(N):
            @pl.when(x != k)
            def _():
                x_copy(g, k).start()

    def b_copy(g):
        z0, n = GROUPS[g]
        ref = cb.at[pl.ds(z0, n), :, c]
        return remote(ref, ref, bs.at[g], br.at[g], sib)

    def b_wait(g):
        z0, n = GROUPS[g]
        ref = cb.at[pl.ds(z0, n), :, 1 - c]
        remote(ref, ref, bs.at[g], br.at[g], sib).wait_recv()

    def share(g):
        for k in range(N):
            @pl.when(x != k)
            def _():
                x_wait(g, k)
        b_copy(g).start()

    share(0)
    own_r.wait()
    for k in (0, 1, 4, 5, 6, 7):
        r_wait(k)
    first_rows = rb[0:4].reshape(B, 2 * 128)
    second_rows = rb[4:8].reshape(B, 2 * 128)
    u = product(load(h_inv1), split(first_rows))
    rest = second_rows - product(load(h_ll), split(u))
    share(1)
    y_two = split(product(load(h_inv2), split(rest)))
    h_y[0, B:], h_y[1, B:] = y_two
    h_y[0, :B], h_y[1, :B] = split(u - product(load(h_n), y_two))
    own_t.wait()

    def eliminate(g):
        z0, n = GROUPS[g]
        k0, kn = z0 * 128, n * 128
        b_wait(g)
        left = cb[z0:z0 + n].reshape(kn, B).T
        return product(split(left), (h_y[0, k0:k0 + kn], h_y[1, k0:k0 + kn]))

    trail[...] = trail[...] - eliminate(0)
    share(2)
    trail[...] = trail[...] - eliminate(1)
    share(3)
    trail[...] = trail[...] - eliminate(2)
    out_ref[...] = trail[...] - eliminate(3)

    for k in range(N):
        @pl.when(z != k)
        def _():
            z_copy(k).wait_send()

        @pl.when(x != k)
        def _():
            for g in range(len(GROUPS)):
                x_copy(g, k).wait_send()

    for k in range(8):
        r_copy(k).wait_send()
    for g in range(len(GROUPS)):
        b_copy(g).wait_send()


def local_step(pivot, col_panel, row_panel, trailing):
    pair = pltpu.VMEM((2, B, B), BF16)
    return pl.pallas_call(
        kernel,
        out_shape=jax.ShapeDtypeStruct(trailing.shape, F32),
        in_specs=[pl.BlockSpec(memory_space=pl.ANY)] * 4,
        out_specs=pl.BlockSpec(memory_space=pltpu.VMEM),
        scratch_shapes=[
            pltpu.VMEM((2 * B, 2 * B), F32),
            pltpu.VMEM((N, 128, 256), F32),
            pltpu.VMEM((N, N, 2, 8, B), F32),
            pltpu.VMEM((B, 256), F32),
            pltpu.VMEM((B, B), F32),
            pltpu.VMEM((B, B), F32),
            pair, pair, pair, pair, pair, pair,
            pltpu.VMEM((2, 2 * B, 256), BF16),
            pltpu.SemaphoreType.DMA((7,)),
            pltpu.SemaphoreType.DMA((N,)),
            pltpu.SemaphoreType.DMA((N,)),
            pltpu.SemaphoreType.DMA((len(GROUPS), N)),
            pltpu.SemaphoreType.DMA((len(GROUPS), N)),
            pltpu.SemaphoreType.DMA((len(GROUPS),)),
            pltpu.SemaphoreType.DMA((len(GROUPS),)),
            pltpu.SemaphoreType.DMA((8,)),
            pltpu.SemaphoreType.DMA((8,)),
            pltpu.SemaphoreType.REGULAR((N,)),
            pltpu.SemaphoreType.REGULAR((N,)),
            pltpu.SemaphoreType.REGULAR((4,)),
            pltpu.SemaphoreType.REGULAR((1,)),
        ],
        compiler_params=pltpu.CompilerParams(collective_id=0, has_side_effects=True, vmem_limit_bytes=56 << 20),
        name="eliminate",
    )(pivot, col_panel.T, row_panel, trailing)


def solution(mesh):
    return jax.shard_map(
        local_step,
        mesh=mesh,
        in_specs=(P(), P("row", "col"), P("row", "col"), P("row", "col")),
        out_specs=P("row", "col"),
        check_vma=False,
    )
```

time: 134 us -> 54.3 us (0.41)
  the two profiles are of different devices: /device:TPU:1 before, /device:TPU:9 now
where the time goes in v1:
time: 54.3 us; the launch traced here: 54.1 us
  Pallas kernels  52.2 us (96%)
  local copies, waits for them, and re-layouts  1.87 us (3%)
    pallas_call x1, Pallas kernels, local_step(): pl.pallas_call(kernel, out_shape=jax.ShapeDtypeStruct(trailing.shape, F32...  52.2 us
    unnamed x1, local copies, waits for them, and re-layouts  1.87 us

profile of v1, /device:TPU:9, one launch (start us, length us, event | category | flops | bytes accessed | tf_op | source)
XLA Modules:
  0.0 54.1 jit_solution(692966646715490313)
XLA Ops:
  0.0 52.2 %eliminate.1 = f32[512,256]{1,0:T(8,128)} custom-call(f32[1024,1024]{1,0:T(8,128)} %pivot_ref.1, f32[8,512]{1,0:T(8,128)} %bitcast.1, f32[128,256]{1,0:T(8,128)} %row_ref.1, f32[512,256]{1,0:T(8,128)} %trail_ref.1), custom_call_target="tpu_custom_call" | custom-call | tf_op jit(solution)/shard_map/eliminate/pallas_call | solution.py:275
  52.2 1.9 %copy.6 = f32[512,256]{1,0:T(8,128)} copy(f32[512,256]{1,0:T(8,128)} %eliminate.1) | data formatting | bytes 1048576

commit v2 on v1

--- a/solution.py
+++ b/solution.py
@@ -10,7 +10,7 @@
 MESH = pl.DeviceIdType.MESH
 F32 = jnp.float32
 BF16 = jnp.bfloat16
-GROUPS = ((0, 4), (4, 2), (6, 1), (7, 1))
+GROUPS = ((0, 2), (2, 2), (4, 1), (5, 1), (6, 1), (7, 1))
 
 
 def split(value):
@@ -27,12 +27,14 @@
 
 
 def kernel(pivot_ref, col_ref, row_ref, trail_ref, out_ref, piv, rb, cb, trail, f_a, f_b, h_a, h_b, h_inv1, h_n, h_ll, h_inv2, h_y,
-           loc, zs, zr, xs, xr, bs, br, rs, rr, inz, inx, iny, ins):
+           loc, ps, pr, xs, xr, zs, zr, bs, br, rs, rr, inz, inx, iny, ins):
     y = lax.axis_index("row")
     col = lax.axis_index("col")
     c = lax.rem(col, 2)
     x = lax.rem(col // 2, N)
     z = col // (2 * N)
+    p = jnp.where(c == 0, z, x)
+    q = jnp.where(c == 0, x, z)
 
     def column(z_, x_, c_):
         return (z_ * N + x_) * 2 + c_
@@ -49,9 +51,10 @@
     for k in range(N):
         zp.append((y, column(k, x, c)))
         partners.append((zp[k], z != k, k + first(y, k, x, c) > z + mine, inz.at[z], inz.at[k]))
-    for k in range(N):
+    for o in range(1, N):
+        k = lax.rem(x + o, N)
         xp.append((y, column(z, k, c)))
-        partners.append((xp[k], x != k, ringed(jnp.int32(k)) + first(y, z, k, c) > ringed(x) + mine, inx.at[x], inx.at[k]))
+        partners.append((xp[-1], None, ringed(k) + first(y, z, k, c) > ringed(x) + mine, inx.at[x], inx.at[k]))
     for k, off in enumerate((1, N - 1, 2, N - 2)):
         other = lax.rem(y + off, N)
         yp.append((other, col))
@@ -63,10 +66,10 @@
         return b if a is None else a & b
 
     local = []
-    for k, (r, q) in enumerate(((0, 0), (0, 1), (1, 0), (1, 1))):
-        part = (pl.ds(r * B, B), pl.ds(q * B, B))
+    for k, (down, right) in enumerate(((0, 0), (0, 1), (1, 0), (1, 1))):
+        part = (pl.ds(down * B, B), pl.ds(right * B, B))
         local.append(pltpu.make_async_copy(pivot_ref.at[part], piv.at[part], loc.at[k]))
-    own_c = pltpu.make_async_copy(col_ref, cb.at[z, x, c], loc.at[4])
+    own_c = pltpu.make_async_copy(col_ref, cb.at[c, p, q], loc.at[4])
     own_r = pltpu.make_async_copy(row_ref, rb.at[y], loc.at[5])
     own_t = pltpu.make_async_copy(trail_ref, trail, loc.at[6])
     own_c.start()
@@ -89,18 +92,29 @@
     def remote(src, dst, send, recv, dev):
         return pltpu.make_async_remote_copy(src_ref=src, dst_ref=dst, send_sem=send, recv_sem=recv, device_id=dev, device_id_type=MESH)
 
-    def z_copy(k, src_z=None):
-        return remote(col_ref, cb.at[z, x, c], zs.at[k], zr.at[z], zp[k])
-
-    def z_wait(k):
-        remote(col_ref, cb.at[k, x, c], zs.at[k], zr.at[k], zp[k]).wait_recv()
+    def first_z(k):
+        return remote(col_ref, cb.at[0, z, x], ps.at[k], pr.at[z], zp[k])
+
+    def first_z_wait(k):
+        remote(col_ref, cb.at[0, k, x], ps.at[k], pr.at[k], zp[k]).wait_recv()
+
+    def first_x(o):
+        return remote(col_ref, cb.at[1, x, z], ps.at[o], pr.at[o], xp[o - 1])
+
+    def first_x_wait(o):
+        remote(col_ref, cb.at[1, lax.rem(x + N - o, N), z], ps.at[o], pr.at[o], xp[o - 1]).wait_recv()
 
     for k in range(N):
         _, there, later, _, _ = partners[k]
 
-        @pl.when(there & jnp.logical_not(later))
-        def _():
-            z_copy(k).start()
+        @pl.when((c == 0) & there & jnp.logical_not(later))
+        def _():
+            first_z(k).start()
+
+    for o in (4, 3, 5, 2, 6, 1, 7):
+        @pl.when((c == 1) & jnp.logical_not(partners[N + o - 1][2]))
+        def _():
+            first_x(o).start()
 
     for dev, there, later, theirs, _ in partners:
         @pl.when(both(there, jnp.logical_not(later)))
@@ -138,9 +152,9 @@
         remote(ref, ref, rs.at[k], rr.at[k], yp[0]).wait_recv()
 
     for k in (2, 3, 0, 1):
-        admit(2 * N + k)
+        admit(2 * N - 1 + k)
         r_copy(k).start()
-    admit(2 * N + 4)
+    admit(2 * N + 3)
 
     eye = (lax.broadcasted_iota(jnp.int32, (B, B), 0) == lax.broadcasted_iota(jnp.int32, (B, B), 1)).astype(F32)
 
@@ -160,73 +174,130 @@
     store(h_inv1, eye + f_a[...] + f_b[...] + product(load(h_a), load(h_b)))
     local[1].wait()
     store(h_n, product(load(h_inv1), split(piv[:B, B:])))
+
+    @pl.when(c == 1)
+    def _():
+        for o in (1, 7, 2, 6, 3, 5, 4):
+            _, _, later, _, own = partners[N + o - 1]
+
+            @pl.when(later)
+            def _():
+                pl.semaphore_wait(own, 1)
+                first_x(o).start()
+
     local[2].wait()
     local[3].wait()
     store(h_ll, piv[B:, :B])
     e = eye - piv[B:, B:] + product(load(h_ll), load(h_n))
     f_a[...] = e
     store(h_a, e)
+
+    def second_z(k):
+        ref = cb.at[1, :, z]
+        return remote(ref, ref, zs.at[k], zr.at[z], zp[k])
+
+    def second_z_wait(k):
+        ref = cb.at[1, :, k]
+        remote(ref, ref, zs.at[k], zr.at[k], zp[k]).wait_recv()
+
+    own_c.wait()
+
+    @pl.when(c == 1)
+    def _():
+        for o in (1, 7, 2, 6, 3, 5, 4):
+            first_x_wait(o)
+        for k in range(N):
+            _, there, later, _, _ = partners[k]
+
+            @pl.when(there & jnp.logical_not(later))
+            def _():
+                second_z(k).start()
+
     r_wait(2)
     r_copy(4).start()
     r_copy(6).start()
     r_wait(3)
     r_copy(5).start()
     r_copy(7).start()
+    def second_x(g, o):
+        z0, n = GROUPS[g]
+        ref = cb.at[0, pl.ds(z0, n), x]
+        return remote(ref, ref, xs.at[g, o - 1], xr.at[g, o - 1], xp[o - 1])
+
+    def second_x_wait(g, o):
+        z0, n = GROUPS[g]
+        ref = cb.at[0, pl.ds(z0, n), lax.rem(x + N - o, N)]
+        remote(ref, ref, xs.at[g, o - 1], xr.at[g, o - 1], xp[o - 1]).wait_recv()
+
+    def pass_on(g):
+        z0, n = GROUPS[g]
+
+        @pl.when(c == 0)
+        def _():
+            for k in range(z0, z0 + n):
+                _, there, later, _, own = partners[k]
+
+                @pl.when(there & later)
+                def _():
+                    pl.semaphore_wait(own, 1)
+                    first_z(k).start()
+
+                @pl.when(there)
+                def _():
+                    first_z_wait(k)
+
+            for o in (4, 3, 5, 2, 6, 1, 7):
+                second_x(g, o).start()
+
+        @pl.when(c == 1)
+        def _():
+            for k in range(z0, z0 + n):
+                _, there, later, _, own = partners[k]
+
+                @pl.when(there & later)
+                def _():
+                    pl.semaphore_wait(own, 1)
+                    second_z(k).start()
+
+    @pl.when(c == 0)
+    def _():
+        for k in range(N - 1):
+            admit(N + k)
+
+    pass_on(0)
+    pass_on(1)
     square = product(load(h_a), load(h_a))
     f_b[...] = square
     store(h_b, square)
     store(h_inv2, eye + f_a[...] + f_b[...] + product(load(h_a), load(h_b)))
 
-    own_c.wait()
-    for k in range(N):
-        admit(N + k)
-
-    def x_copy(g, k):
-        z0, n = GROUPS[g]
-        ref = cb.at[pl.ds(z0, n), x, c]
-        return remote(ref, ref, xs.at[g, k], xr.at[g, x], xp[k])
-
-    def x_wait(g, k):
-        z0, n = GROUPS[g]
-        ref = cb.at[pl.ds(z0, n), k, c]
-        remote(ref, ref, xs.at[g, k], xr.at[g, k], xp[k]).wait_recv()
-
-    for g, (z0, n) in enumerate(GROUPS):
-        for k in range(z0, z0 + n):
-            _, there, later, _, own = partners[k]
-
-            @pl.when(there & later)
-            def _():
-                pl.semaphore_wait(own, 1)
-                z_copy(k).start()
-
-            @pl.when(there)
-            def _():
-                z_wait(k)
-
-        for k in range(N):
-            @pl.when(x != k)
-            def _():
-                x_copy(g, k).start()
-
-    def b_copy(g):
-        z0, n = GROUPS[g]
-        ref = cb.at[pl.ds(z0, n), :, c]
+    for g in range(2, len(GROUPS)):
+        pass_on(g)
+
+    def third(g, core):
+        z0, n = GROUPS[g]
+        ref = cb.at[0, pl.ds(z0, n)] if core == 0 else cb.at[1, :, pl.ds(z0, n)]
         return remote(ref, ref, bs.at[g], br.at[g], sib)
 
-    def b_wait(g):
-        z0, n = GROUPS[g]
-        ref = cb.at[pl.ds(z0, n), :, 1 - c]
-        remote(ref, ref, bs.at[g], br.at[g], sib).wait_recv()
-
     def share(g):
-        for k in range(N):
-            @pl.when(x != k)
-            def _():
-                x_wait(g, k)
-        b_copy(g).start()
+        z0, n = GROUPS[g]
+
+        @pl.when(c == 0)
+        def _():
+            for o in (1, 7, 2, 6, 3, 5, 4):
+                second_x_wait(g, o)
+            third(g, 0).start()
+
+        @pl.when(c == 1)
+        def _():
+            for k in range(z0, z0 + n):
+                @pl.when(z != k)
+                def _():
+                    second_z_wait(k)
+            third(g, 1).start()
 
     share(0)
+    share(1)
     own_r.wait()
     for k in (0, 1, 4, 5, 6, 7):
         r_wait(k)
@@ -234,7 +305,7 @@
     second_rows = rb[4:8].reshape(B, 2 * 128)
     u = product(load(h_inv1), split(first_rows))
     rest = second_rows - product(load(h_ll), split(u))
-    share(1)
+    share(2)
     y_two = split(product(load(h_inv2), split(rest)))
     h_y[0, B:], h_y[1, B:] = y_two
     h_y[0, :B], h_y[1, :B] = split(u - product(load(h_n), y_two))
@@ -243,31 +314,58 @@
     def eliminate(g):
         z0, n = GROUPS[g]
         k0, kn = z0 * 128, n * 128
-        b_wait(g)
-        left = cb[z0:z0 + n].reshape(kn, B).T
+
+        @pl.when(c == 0)
+        def _():
+            third(g, 1).wait_recv()
+
+        @pl.when(c == 1)
+        def _():
+            third(g, 0).wait_recv()
+
+        blocks = []
+        for a in range(z0, z0 + n):
+            for b in range(N):
+                blocks += [cb[0, a, b], cb[1, b, a]]
+        left = jnp.concatenate(blocks, axis=0).T
         return product(split(left), (h_y[0, k0:k0 + kn], h_y[1, k0:k0 + kn]))
 
     trail[...] = trail[...] - eliminate(0)
-    share(2)
+    share(3)
     trail[...] = trail[...] - eliminate(1)
-    share(3)
+    share(4)
     trail[...] = trail[...] - eliminate(2)
-    out_ref[...] = trail[...] - eliminate(3)
-
-    for k in range(N):
-        @pl.when(z != k)
-        def _():
-            z_copy(k).wait_send()
-
-        @pl.when(x != k)
-        def _():
-            for g in range(len(GROUPS)):
-                x_copy(g, k).wait_send()
+    share(5)
+    trail[...] = trail[...] - eliminate(3)
+    trail[...] = trail[...] - eliminate(4)
+    out_ref[...] = trail[...] - eliminate(5)
 
     for k in range(8):
         r_copy(k).wait_send()
-    for g in range(len(GROUPS)):
-        b_copy(g).wait_send()
+
+    @pl.when(c == 0)
+    def _():
+        for k in range(N):
+            @pl.when(z != k)
+            def _():
+                first_z(k).wait_send()
+
+        for g in range(len(GROUPS)):
+            for o in range(1, N):
+                second_x(g, o).wait_send()
+            third(g, 0).wait_send()
+
+    @pl.when(c == 1)
+    def _():
+        for o in range(1, N):
+            first_x(o).wait_send()
+        for k in range(N):
+            @pl.when(z != k)
+            def _():
+                second_z(k).wait_send()
+
+        for g in range(len(GROUPS)):
+            third(g, 1).wait_send()
 
 
 def local_step(pivot, col_panel, row_panel, trailing):
@@ -280,7 +378,7 @@
         scratch_shapes=[
             pltpu.VMEM((2 * B, 2 * B), F32),
             pltpu.VMEM((N, 128, 256), F32),
-            pltpu.VMEM((N, N, 2, 8, B), F32),
+            pltpu.VMEM((2, N, N, 8, B), F32),
             pltpu.VMEM((B, 256), F32),
             pltpu.VMEM((B, B), F32),
             pltpu.VMEM((B, B), F32),
@@ -291,6 +389,8 @@
             pltpu.SemaphoreType.DMA((N,)),
             pltpu.SemaphoreType.DMA((len(GROUPS), N)),
             pltpu.SemaphoreType.DMA((len(GROUPS), N)),
+            pltpu.SemaphoreType.DMA((N,)),
+            pltpu.SemaphoreType.DMA((N,)),
             pltpu.SemaphoreType.DMA((len(GROUPS),)),
             pltpu.SemaphoreType.DMA((len(GROUPS),)),
             pltpu.SemaphoreType.DMA((8,)),

time: 54.3 us -> 47.2 us (0.87)
  the two profiles are of different devices: /device:TPU:9 before, /device:TPU:897 now
where the time goes in v2:
time: 47.2 us; the launch traced here: 47 us
  Pallas kernels  45.1 us (96%)
  local copies, waits for them, and re-layouts  1.87 us (4%)
    pallas_call x1, Pallas kernels, local_step(): pl.pallas_call(kernel, out_shape=jax.ShapeDtypeStruct(trailing.shape, F32...  45.1 us
    unnamed x1, local copies, waits for them, and re-layouts  1.87 us

profile of v2, /device:TPU:897, one launch (start us, length us, event | category | flops | bytes accessed | tf_op | source)
XLA Modules:
  0.0 47.0 jit_solution(9029293353328341735)
XLA Ops:
  0.0 45.1 %eliminate.1 = f32[512,256]{1,0:T(8,128)} custom-call(f32[1024,1024]{1,0:T(8,128)} %pivot_ref.1, f32[8,512]{1,0:T(8,128)} %bitcast.1, f32[128,256]{1,0:T(8,128)} %row_ref.1, f32[512,256]{1,0:T(8,128)} %trail_ref.1), custom_call_target="tpu_custom_call" | custom-call | tf_op jit(solution)/shard_map/eliminate/pallas_call | solution.py:373
  45.1 1.9 %copy.6 = f32[512,256]{1,0:T(8,128)} copy(f32[512,256]{1,0:T(8,128)} %eliminate.1) | data formatting | bytes 1048576

commit v3 on v2

--- a/solution.py
+++ b/solution.py
@@ -50,7 +50,8 @@
     zp, xp, yp = [], [], []
     for k in range(N):
         zp.append((y, column(k, x, c)))
-        partners.append((zp[k], z != k, k + first(y, k, x, c) > z + mine, inz.at[z], inz.at[k]))
+        apart = lax.rem(z + N - k, N)
+        partners.append((zp[k], (z != k) & ((c == 0) | (apart == 1) | (apart == N - 1)), k + first(y, k, x, c) > z + mine, inz.at[z], inz.at[k]))
     for o in range(1, N):
         k = lax.rem(x + o, N)
         xp.append((y, column(z, k, c)))
@@ -192,13 +193,33 @@
     f_a[...] = e
     store(h_a, e)
 
-    def second_z(k):
-        ref = cb.at[1, :, z]
-        return remote(ref, ref, zs.at[k], zr.at[z], zp[k])
-
-    def second_z_wait(k):
+    def slot_of(step, way):
+        return lax.rem(z + (N - step if way == 0 else step), N)
+
+    def ring_ref(slot, step, way):
+        return cb.at[1, :, slot] if step < 4 else cb.at[1, pl.ds(4 * way, 4), slot]
+
+    def ring(way, step):
+        ref = ring_ref(slot_of(step - 1, way), step, way)
+        dev = (y, column(lax.rem(z + (1, N - 1)[way], N), x, c))
+        at = 4 * way + step - 1
+        return remote(ref, ref, zs.at[at], zr.at[at], dev)
+
+    def ring_step(way, step):
+        ref = ring_ref(slot_of(step, way), step, way)
+        at = 4 * way + step - 1
+        remote(ref, ref, zs.at[at], zr.at[at], sib).wait_recv()
+        if step < 4:
+            ring(way, step + 1).start()
+
+    def third_x(g):
+        z0, n = GROUPS[g]
+        ref = cb.at[0, pl.ds(z0, n)]
+        return remote(ref, ref, bs.at[g], br.at[g], sib)
+
+    def third_z(k):
         ref = cb.at[1, :, k]
-        remote(ref, ref, zs.at[k], zr.at[k], zp[k]).wait_recv()
+        return remote(ref, ref, bs.at[k], br.at[k], sib)
 
     own_c.wait()
 
@@ -206,12 +227,17 @@
     def _():
         for o in (1, 7, 2, 6, 3, 5, 4):
             first_x_wait(o)
-        for k in range(N):
-            _, there, later, _, _ = partners[k]
-
-            @pl.when(there & jnp.logical_not(later))
-            def _():
-                second_z(k).start()
+        @pl.when(z != N - 1)
+        def _():
+            pl.semaphore_wait(inz.at[z + 1], 1)
+
+        ring(0, 1).start()
+
+        @pl.when(z != 0)
+        def _():
+            ring(1, 1).start()
+
+        third_z(z).start()
 
     r_wait(2)
     r_copy(4).start()
@@ -249,16 +275,6 @@
             for o in (4, 3, 5, 2, 6, 1, 7):
                 second_x(g, o).start()
 
-        @pl.when(c == 1)
-        def _():
-            for k in range(z0, z0 + n):
-                _, there, later, _, own = partners[k]
-
-                @pl.when(there & later)
-                def _():
-                    pl.semaphore_wait(own, 1)
-                    second_z(k).start()
-
     @pl.when(c == 0)
     def _():
         for k in range(N - 1):
@@ -274,27 +290,29 @@
     for g in range(2, len(GROUPS)):
         pass_on(g)
 
-    def third(g, core):
-        z0, n = GROUPS[g]
-        ref = cb.at[0, pl.ds(z0, n)] if core == 0 else cb.at[1, :, pl.ds(z0, n)]
-        return remote(ref, ref, bs.at[g], br.at[g], sib)
+    @pl.when(c == 1)
+    def _():
+        @pl.when(z == 0)
+        def _():
+            pl.semaphore_wait(inz.at[N - 1], 1)
+            ring(1, 1).start()
+
+        for step in range(1, 4):
+            @pl.when(z >= 4 + step)
+            def _():
+                ring_step(0, step)
+
+        for step in range(1, 5):
+            ring_step(1, step)
+            if step < 4:
+                third_z(slot_of(step, 1)).start()
 
     def share(g):
-        z0, n = GROUPS[g]
-
         @pl.when(c == 0)
         def _():
             for o in (1, 7, 2, 6, 3, 5, 4):
                 second_x_wait(g, o)
-            third(g, 0).start()
-
-        @pl.when(c == 1)
-        def _():
-            for k in range(z0, z0 + n):
-                @pl.when(z != k)
-                def _():
-                    second_z_wait(k)
-            third(g, 1).start()
+            third_x(g).start()
 
     share(0)
     share(1)
@@ -310,19 +328,27 @@
     h_y[0, B:], h_y[1, B:] = y_two
     h_y[0, :B], h_y[1, :B] = split(u - product(load(h_n), y_two))
     own_t.wait()
-
-    def eliminate(g):
-        z0, n = GROUPS[g]
+    for g in range(3, len(GROUPS)):
+        share(g)
+
+    @pl.when(c == 1)
+    def _():
+        for step in range(1, 5):
+            @pl.when(z < 4 + step)
+            def _():
+                ring_step(0, step)
+
+            third_z(slot_of(step, 0)).start()
+        for g in range(len(GROUPS)):
+            third_x(g).wait_recv()
+
+    @pl.when(c == 0)
+    def _():
+        for k in range(N):
+            third_z(k).wait_recv()
+
+    def eliminate(z0, n):
         k0, kn = z0 * 128, n * 128
-
-        @pl.when(c == 0)
-        def _():
-            third(g, 1).wait_recv()
-
-        @pl.when(c == 1)
-        def _():
-            third(g, 0).wait_recv()
-
         blocks = []
         for a in range(z0, z0 + n):
             for b in range(N):
@@ -330,15 +356,8 @@
         left = jnp.concatenate(blocks, axis=0).T
         return product(split(left), (h_y[0, k0:k0 + kn], h_y[1, k0:k0 + kn]))
 
-    trail[...] = trail[...] - eliminate(0)
-    share(3)
-    trail[...] = trail[...] - eliminate(1)
-    share(4)
-    trail[...] = trail[...] - eliminate(2)
-    share(5)
-    trail[...] = trail[...] - eliminate(3)
-    trail[...] = trail[...] - eliminate(4)
-    out_ref[...] = trail[...] - eliminate(5)
+    trail[...] = trail[...] - eliminate(0, 4)
+    out_ref[...] = trail[...] - eliminate(4, 4)
 
     for k in range(8):
         r_copy(k).wait_send()
@@ -353,19 +372,17 @@
         for g in range(len(GROUPS)):
             for o in range(1, N):
                 second_x(g, o).wait_send()
-            third(g, 0).wait_send()
+            third_x(g).wait_send()
 
     @pl.when(c == 1)
     def _():
         for o in range(1, N):
             first_x(o).wait_send()
+        for step in range(1, 5):
+            ring(0, step).wait_send()
+            ring(1, step).wait_send()
         for k in range(N):
-            @pl.when(z != k)
-            def _():
-                second_z(k).wait_send()
-
-        for g in range(len(GROUPS)):
-            third(g, 1).wait_send()
+            third_z(k).wait_send()
 
 
 def local_step(pivot, col_panel, row_panel, trailing):
@@ -391,8 +408,8 @@
             pltpu.SemaphoreType.DMA((len(GROUPS), N)),
             pltpu.SemaphoreType.DMA((N,)),
             pltpu.SemaphoreType.DMA((N,)),
-            pltpu.SemaphoreType.DMA((len(GROUPS),)),
-            pltpu.SemaphoreType.DMA((len(GROUPS),)),
+            pltpu.SemaphoreType.DMA((N,)),
+            pltpu.SemaphoreType.DMA((N,)),
             pltpu.SemaphoreType.DMA((8,)),
             pltpu.SemaphoreType.DMA((8,)),
             pltpu.SemaphoreType.REGULAR((N,)),

time: 47.2 us -> 51.1 us (1.083)
  the two profiles are of different devices: /device:TPU:897 before, /device:TPU:134 now
where the time goes in v3:
time: 51.1 us; the launch traced here: 50.9 us
  Pallas kernels  49 us (96%)
  local copies, waits for them, and re-layouts  1.87 us (4%)
    pallas_call x1, Pallas kernels, local_step(): pl.pallas_call(kernel, out_shape=jax.ShapeDtypeStruct(trailing.shape, F32...  49 us
    unnamed x1, local copies, waits for them, and re-layouts  1.87 us

profile of v3, /device:TPU:134, one launch (start us, length us, event | category | flops | bytes accessed | tf_op | source)
XLA Modules:
  0.0 50.9 jit_solution(12882649534594876759)
XLA Ops:
  0.0 49.0 %eliminate.1 = f32[512,256]{1,0:T(8,128)} custom-call(f32[1024,1024]{1,0:T(8,128)} %pivot_ref.1, f32[8,512]{1,0:T(8,128)} %bitcast.1, f32[128,256]{1,0:T(8,128)} %row_ref.1, f32[512,256]{1,0:T(8,128)} %trail_ref.1), custom_call_target="tpu_custom_call" | custom-call | tf_op jit(solution)/shard_map/eliminate/pallas_call | solution.py:390
  49.1 1.9 %copy.6 = f32[512,256]{1,0:T(8,128)} copy(f32[512,256]{1,0:T(8,128)} %eliminate.1) | data formatting | bytes 1048576

commit v4 on v2

--- a/solution.py
+++ b/solution.py
@@ -247,7 +247,19 @@
                     first_z_wait(k)
 
             for o in (4, 3, 5, 2, 6, 1, 7):
-                second_x(g, o).start()
+                if g == 0:
+                    @pl.when(jnp.logical_not(partners[N + o - 1][2]))
+                    def _():
+                        second_x(g, o).start()
+                else:
+                    second_x(g, o).start()
+
+            if g == 0:
+                for o in (1, 7, 2, 6, 3, 5, 4):
+                    @pl.when(partners[N + o - 1][2])
+                    def _():
+                        pl.semaphore_wait(partners[N + o - 1][4], 1)
+                        second_x(g, o).start()
 
         @pl.when(c == 1)
         def _():
@@ -258,11 +270,6 @@
                 def _():
                     pl.semaphore_wait(own, 1)
                     second_z(k).start()
-
-    @pl.when(c == 0)
-    def _():
-        for k in range(N - 1):
-            admit(N + k)
 
     pass_on(0)
     pass_on(1)

time: 47.2 us -> 46.3 us (0.981)
  Pallas kernels: 45.1 us -> 44.2 us
    pallas_call x1, Pallas kernels: 45.1 us -> 44.2 us  [local_step(): pl.pallas_call(kernel, out_shape=jax.ShapeDtypeStruct(trailing.shape, F32...]
where the time goes in v4:
time: 46.3 us; the launch traced here: 46.1 us
  Pallas kernels  44.2 us (95%)
  local copies, waits for them, and re-layouts  1.87 us (4%)
    pallas_call x1, Pallas kernels, local_step(): pl.pallas_call(kernel, out_shape=jax.ShapeDtypeStruct(trailing.shape, F32...  44.2 us
    unnamed x1, local copies, waits for them, and re-layouts  1.87 us

profile of v4, /device:TPU:897, one launch (start us, length us, event | category | flops | bytes accessed | tf_op | source)
XLA Modules:
  0.0 46.1 jit_solution(4654936600216121215)
XLA Ops:
  0.0 44.2 %eliminate.1 = f32[512,256]{1,0:T(8,128)} custom-call(f32[1024,1024]{1,0:T(8,128)} %pivot_ref.1, f32[8,512]{1,0:T(8,128)} %bitcast.1, f32[128,256]{1,0:T(8,128)} %row_ref.1, f32[512,256]{1,0:T(8,128)} %trail_ref.1), custom_call_target="tpu_custom_call" | custom-call | tf_op jit(solution)/shard_map/eliminate/pallas_call | solution.py:380
  44.2 1.9 %copy.6 = f32[512,256]{1,0:T(8,128)} copy(f32[512,256]{1,0:T(8,128)} %eliminate.1) | data formatting | bytes 1048576
